TPU v7x, 256 devices: a whole 4x4x8 slice. The times are simulated.
256 devices in a mesh: pool: 2 (over z_hi), grp: 16 (over z_lo, x), cuts: 8 (over y, core).
Axes of the slice: x: 4, y: 4, z: 8 (z_hi: 2, z_lo: 4; z = z_hi * 4 + z_lo), core: 2. Of those that a mesh axis runs over, the one named last changes fastest.
Arguments:
- residual_in: bfloat16 [1024, 6144], P(('pool', 'grp'), 'cuts'), may hold values from -64 to 64
- queries: bfloat16 [1024, 6144], P(('pool', 'grp'), 'cuts'), may hold values from -1024 to 1024
- key_new: bfloat16 [1024, 1024], P(('pool', 'grp'), 'cuts'), may hold values from -5 to 5
- value_new: bfloat16 [1024, 1024], P(('pool', 'grp'), 'cuts'), may hold values from -5 to 5
- key_cache: bfloat16 [1024, 128, 1024], P(('pool', 'grp'), None, 'cuts'), may hold values from -8 to 8
- value_cache: bfloat16 [1024, 128, 1024], P(('pool', 'grp'), None, 'cuts'), may hold values from -5 to 5
- cache_lens: int32 [1024], P(('pool', 'grp')), may hold values from 2 to 128, as said below
- norm_gain: float32 [6144], replicated, may hold values from 0.1 to 1.9
- expert_ids: int32 [1024, 4], P(('pool', 'grp')), may hold values from 0 to 15, all different within a row; in each aligned block of 32 rows (0 to 31, 32 to 63, ...) at most 16 rows name the same one
- gate_weights: float32 [1024, 4], P(('pool', 'grp')), may hold values from 0.1 to 0.6
- w_in: bfloat16 [16, 6144, 6144], P('grp', None, ('pool', 'cuts')), may hold values from -0.078125 to 0.078125
- w_out: bfloat16 [16, 6144, 6144], P('grp', ('pool', 'cuts')), may hold values from -0.078125 to 0.078125
Outputs:
- attended: bfloat16 [1024, 6144], P(('pool', 'grp'), 'cuts')
- expert_mix: bfloat16 [1024, 6144], P(('pool', 'grp'), 'cuts')
Inputs may be any that keep to these rules, and one draw needn't show every extreme that they name: `expert_ids`: each row names 4 different experts; among the rows of one attention group (32 rows in order) no expert is named more than 16 times, a bound that some block reaches. `cache_lens`: the first row of every attention group has 128 live entries.
All inputs are finite; a program needn't handle non-finite values.
Results may differ from a plain program's by a relative error of at most 0.022.
Values may be sent and summed in bfloat16 or wider, within the bound.
A program may use at most 128 MiB of HBM per device.

v0:
```python
import math

import jax
import jax.numpy as jnp
from jax import lax
from jax.sharding import PartitionSpec as P

HEAD_DIM = 128
EXP_DEV = 1


def attend_local(queries, key_new, value_new, key_cache, value_cache, cache_lens):
    row_count = queries.shape[0]
    kv_count = key_cache.shape[-1] // HEAD_DIM
    group_size = queries.shape[-1] // key_cache.shape[-1]
    key_span = key_cache.shape[1]
    query_part = queries.reshape(row_count, kv_count, group_size, HEAD_DIM)
    keys_part = key_cache.reshape(row_count, key_span, kv_count, HEAD_DIM)
    values_part = value_cache.reshape(row_count, key_span, kv_count, HEAD_DIM)
    knew_part = key_new.reshape(row_count, kv_count, HEAD_DIM)
    vnew_f = value_new.astype(jnp.float32).reshape(row_count, kv_count, HEAD_DIM)
    score_scale = 1.0 / math.sqrt(HEAD_DIM)
    scores = (
        jnp.einsum("rkgd,rtkd->rkgt", query_part, keys_part, preferred_element_type=jnp.float32)
        * score_scale
    )
    own_score = (
        jnp.einsum("rkgd,rkd->rkg", query_part, knew_part, preferred_element_type=jnp.float32)
        * score_scale
    )
    live_mask = (jnp.arange(key_span, dtype=jnp.int32)[None, :] < cache_lens[:, None])[
        :, None, None, :
    ]
    scores = jnp.where(live_mask, scores, -1e30)
    row_peak = jnp.maximum(jnp.max(scores, axis=-1), own_score)
    raw_weights = jnp.where(live_mask, jnp.exp(scores - row_peak[..., None]), 0.0)
    own_weight = jnp.exp(own_score - row_peak)
    denominator = jnp.sum(raw_weights, axis=-1) + own_weight
    key_probs = (raw_weights / denominator[..., None]).astype(jnp.bfloat16)
    own_prob = (own_weight / denominator).astype(jnp.bfloat16)
    head_output = jnp.einsum(
        "rkgt,rtkd->rkgd", key_probs, values_part, preferred_element_type=jnp.float32
    )
    head_output = head_output + own_prob.astype(jnp.float32)[..., None] * vnew_f[:, :, None, :]
    return head_output.reshape(row_count, -1).astype(jnp.bfloat16)


def body(
    residual_in,
    queries,
    key_new,
    value_new,
    key_cache,
    value_cache,
    cache_lens,
    norm_gain,
    expert_ids,
    gate_weights,
    w_in,
    w_out,
):
    attended = attend_local(queries, key_new, value_new, key_cache, value_cache, cache_lens)
    stream = (residual_in.astype(jnp.float32) + attended.astype(jnp.float32)).astype(jnp.bfloat16)
    row_count = stream.shape[0]
    cut_count = lax.axis_size("cuts")
    expert_count = lax.axis_size("grp") * EXP_DEV
    top_count = expert_ids.shape[1]
    capacity = min(row_count, 2 * row_count * top_count // expert_count)
    picks = expert_ids[:, :, None] == jnp.arange(expert_count, dtype=jnp.int32)[None, None, :]
    chosen = jnp.sum(picks.astype(jnp.int32), axis=1)
    weight_table = jnp.sum(jnp.where(picks, gate_weights[:, :, None], 0.0), axis=1)
    slot_index = jnp.cumsum(chosen, axis=0) - chosen
    dispatch = (chosen[:, :, None] == 1) & (
        slot_index[:, :, None] == jnp.arange(capacity, dtype=jnp.int32)[None, None, :]
    )
    dispatch_bf = dispatch.astype(jnp.bfloat16)
    full_rows = lax.all_gather(stream, "cuts", axis=1, tiled=True)
    full_f = full_rows.astype(jnp.float32)
    mean_val = jnp.mean(full_f, axis=-1, keepdims=True)
    mean_sq = jnp.mean(full_f * full_f, axis=-1, keepdims=True)
    variance = mean_sq - mean_val * mean_val
    normed = ((full_f - mean_val) * lax.rsqrt(variance + 1e-05) * norm_gain).astype(jnp.bfloat16)
    outgoing = jnp.einsum(
        "rec,rd->ecd", dispatch_bf, normed, preferred_element_type=jnp.float32
    ).astype(jnp.bfloat16)
    arrived = lax.all_to_all(outgoing, "grp", split_axis=0, concat_axis=0, tiled=True)
    weight_in = w_in[0]
    inner = jnp.einsum(
        "psnd,dh->psnh",
        lax.all_gather(arrived[None], "pool", axis=0, tiled=True),
        weight_in,
        preferred_element_type=jnp.float32,
    )
    hidden = jax.nn.silu(inner).astype(jnp.bfloat16)
    ff_local = w_out.shape[1]
    width_all = w_out.shape[2]
    col_width = width_all // cut_count
    out_table = w_out[0].reshape(ff_local, cut_count, col_width)
    targets = jnp.arange(1 * lax.axis_size(("pool", "cuts")), dtype=jnp.int32)
    pool_pick = targets // cut_count
    cut_pick = targets % cut_count
    hidden_sel = jnp.take(hidden, pool_pick, axis=0)
    table_sel = jnp.take(out_table, cut_pick, axis=1)
    reduced = lax.psum_scatter(
        jnp.einsum(
            "jsnh,hjd->jsnd", hidden_sel, table_sel, preferred_element_type=jnp.float32
        ).astype(jnp.bfloat16),
        ("pool", "cuts"),
        scatter_dimension=0,
        tiled=True,
    ).astype(jnp.float32)
    returned = lax.all_to_all(
        reduced[0].astype(jnp.bfloat16), "grp", split_axis=0, concat_axis=0, tiled=True
    )
    combine = dispatch.astype(jnp.float32) * weight_table[:, :, None]
    expert_mix = jnp.einsum(
        "rec,ecd->rd", combine, returned.astype(jnp.float32), precision=lax.Precision.HIGHEST
    )
    return (attended, expert_mix.astype(jnp.bfloat16))


def solution(mesh):
    return jax.shard_map(
        body,
        mesh=mesh,
        in_specs=(
            P(("pool", "grp"), "cuts"),
            P(("pool", "grp"), "cuts"),
            P(("pool", "grp"), "cuts"),
            P(("pool", "grp"), "cuts"),
            P(("pool", "grp"), None, "cuts"),
            P(("pool", "grp"), None, "cuts"),
            P(("pool", "grp")),
            P(),
            P(("pool", "grp"), None),
            P(("pool", "grp"), None),
            P("grp", None, ("pool", "cuts")),
            P("grp", ("pool", "cuts"), None),
        ),
        out_specs=(P(("pool", "grp"), "cuts"), P(("pool", "grp"), "cuts")),
        check_vma=False,
    )
```

profile of v0, /device:TPU:2, one launch (start us, length us, event | category | flops | bytes accessed | tf_op | source)
XLA Modules:
  0.0 430.0 jit_solution(6518948688003980387)
XLA Ops:
  7.2 0.0 copy-start
  7.2 0.0 all-gather.3.cloned.1.call-start
  7.2 0.8 convert_reduce_fusion.1
  8.0 0.1 copy.42
  8.1 0.7 iota_compare_fusion.2
  8.8 0.9 reshape.199
  9.7 0.9 fusion.38
  10.5 0.0 copy-done
  10.6 0.7 fusion.48
  11.3 0.2 fusion.31
  11.5 0.7 convert_element_type.62
  12.2 1.7 fusion.14
  13.9 1.4 add_convert_fusion
  15.3 13.5 %all_gather.6 = bf16[32,6144]{1,0:T(8,128)(2,1)S(1)} all-gather(bf16[32,768]{1,0:T(8,128)(2,1)S(1)} %get-tuple-element.4), channel_id=1, replica_groups=mesh['pool'=2,'grp'=16,'cuts'=8] {'cuts'}, dimensions={1}, use_global_device_ids=true | all-gather | bytes 442368 | tf_op jit(solution)/shard_map/all_gather | solution.py:77
  28.8 0.2 convert_reduce_fusion
  29.0 0.1 reduce_window_sum.11
  29.1 0.1 copy.44
  29.2 1.8 convolution_convert_fusion
  31.0 79.1 %all_to_all.10 = bf16[16,16,6144]{2,1,0:T(8,128)(2,1)} all-to-all(bf16[16,16,6144]{2,1,0:T(8,128)(2,1)S(1)} %convolution_convert_fusion), channel_id=1, replica_groups=mesh['pool'=2,'grp'=16,'cuts'=8] {'grp'}, dimensions={0} | all-to-all | bytes 6291456 | tf_op jit(solution)/shard_map/all_to_all | solution.py:86
  110.1 0.0 all-gather.3.cloned.1.call-update
  110.1 0.0 reduce-scatter.2.cloned.1.call-start
  110.2 6.6 %copy.46 = bf16[1,384,6144]{1,2,0:T(8,128)(2,1)} copy(bf16[1,384,6144]{2,1,0:T(8,128)(2,1)} %param.23) | data formatting | bytes 9437184 | tf_op args[11]
  116.8 6.7 %copy.47 = bf16[384,8,768]{2,0,1:T(8,128)(2,1)} copy(bf16[384,8,768]{0,2,1:T(8,128)(2,1)} %bitcast.44) | data formatting | bytes 9437184 | tf_op jit(solution)/shard_map/reshape;squeeze | solution.py:98
  123.5 8.2 %gather_fusion.1 = bf16[16,384,768]{2,1,0:T(8,128)(2,1)} fusion(bf16[384,8,768]{2,0,1:T(8,128)(2,1)} %copy.47, s32[1024]{0:T(1024)S(1)} %pad_clamp_fusion), kind=kCustom, calls=%fused_computation.1 | custom fusion | bytes 18874432 | tf_op jit(solution)/shard_map/jit(_take)/gather | solution.py:103
  131.8 136.7 %all-gather.3.cloned.1.call-done = bf16[32,16,6144]{2,1,0:T(8,128)(2,1)} async-done(((bf16[16,16,6144]{2,1,0:T(8,128)(2,1)}), bf16[32,16,6144]{2,1,0:T(8,128)(2,1)}) %all-gather.3.cloned.1.call-update) | async-done | bytes 6291472 | tf_op jit(solution)/shard_map/all_gather | solution.py:90
  268.5 7.6 %multiply_convert_fusion = bf16[2,16,16,384]{3,2,1,0:T(8,128)(2,1)S(1)} fusion(bf16[2,16,16,6144]{3,2,1,0:T(8,128)(2,1)} %bitcast.49, bf16[1,6144,384]{2,1,0:T(8,128)(2,1)} %param.22), kind=kOutput, calls=%fused_computation.27 | convolution fusion | flops 2416902144 | bytes 11403264 | tf_op jit(solution)/shard_map/psnd,dh->psnh/dot_general | solution.py:88
  276.2 2.7 gather_fusion
  278.8 10.9 %fusion.7 = bf16[16,16,16,768]{3,2,1,0:T(8,128)(2,1)} fusion(bf16[16,384,768]{2,1,0:T(8,128)(2,1)} %gather_fusion.1, pred[16]{0:T(512)(128)(4,1)S(1)} %get-tuple-element.12, bf16[16,16,16,384]{3,2,1,0:T(8,128)(2,1)} %gather_fusion, pred[16]{0:T(512)(128)(4,1)S(1)} %get-tuple-element.13), kind=kOutput, calls=%fused_computation.10 | convolution fusion | flops 2425356288 | bytes 18874400 | tf_op jit(solution)/shard_map/jsnh,hjd->jsnd/dot_general | solution.py:105
  289.7 0.0 copy-start.1
  289.7 0.0 copy-start.2
  289.7 0.0 reduce-scatter.2.cloned.1.call-update
  289.7 117.0 %reduce-scatter.2.cloned.1.call-done = bf16[1,16,16,768]{3,2,1,0:T(8,128)(2,1)} async-done(((bf16[16,16,16,768]{3,2,1,0:T(8,128)(2,1)}), bf16[1,16,16,768]{3,2,1,0:T(8,128)(2,1)}) %reduce-scatter.2.cloned.1.call-update) | async-done | bytes 393232 | tf_op jit(solution)/shard_map/reduce_scatter | solution.py:104
  406.7 5.2 %all-to-all-start.1 = ((bf16[16,16,768]{2,1,0:T(8,128)(2,1)}), bf16[16,16,768]{2,1,0:T(8,128)(2,1)S(1)}, u32[]{:S(2)}, u32[]{:S(2)}) async-start(bf16[16,16,768]{2,1,0:T(8,128)(2,1)} %bitcast.45), calls=%async_computation.2 | async-start | bytes 786432 | tf_op jit(solution)/shard_map/all_to_all | solution.py:112
  411.9 0.0 copy-done.1
  411.9 0.0 copy-done.2
  411.9 10.2 %all-to-all-done.1 = bf16[16,16,768]{2,1,0:T(8,128)(2,1)S(1)} async-done(((bf16[16,16,768]{2,1,0:T(8,128)(2,1)}), bf16[16,16,768]{2,1,0:T(8,128)(2,1)S(1)}, u32[]{:S(2)}, u32[]{:S(2)}) %all-to-all-start.1) | async-done | bytes 393248 | tf_op jit(solution)/shard_map/all_to_all | solution.py:112
  422.1 1.0 fusion.15
  (12 shorter events, 0.1 us)
Async XLA Ops:
  7.2 3.4 copy-start
  7.2 261.3 %all-gather.3.cloned.1.call-start = ((), (), s32[]{:S(2)}) async-start(), calls=%async_computation.4 | async-start | bytes 9437184 | tf_op jit(solution)/shard_map/all_gather | solution.py:90
  110.1 296.6 %reduce-scatter.2.cloned.1.call-start = ((), (), s32[]{:S(2)}) async-start(), calls=%async_computation.3 | async-start | bytes 6684672 | tf_op jit(solution)/shard_map/reduce_scatter | solution.py:104
  289.7 122.2 %copy-start.1 = (s32[32,4]{0,1:T(4,128)S(1)}, s32[32,4]{0,1:T(4,128)}, u32[]{:S(2)}) copy-start(s32[32,4]{0,1:T(4,128)} %param.20) | copy-start | bytes 1540
  289.7 122.2 %copy-start.2 = (f32[32,4]{0,1:T(4,128)S(1)}, f32[32,4]{0,1:T(4,128)}, u32[]{:S(2)}) copy-start(f32[32,4]{0,1:T(4,128)} %param.21) | copy-start | bytes 1540
  406.7 15.5 %all-to-all-start.1 = ((bf16[16,16,768]{2,1,0:T(8,128)(2,1)}), bf16[16,16,768]{2,1,0:T(8,128)(2,1)S(1)}, u32[]{:S(2)}, u32[]{:S(2)}) async-start(bf16[16,16,768]{2,1,0:T(8,128)(2,1)} %bitcast.45), calls=%async_computation.2 | async-start | bytes 786432 | tf_op jit(solution)/shard_map/all_to_all | solution.py:112
Sparse Core Ops, SparseCore 0:
  110.2 158.2 all-gather.2
  289.8 116.8 reduce-scatter.1
where the time goes:
time: 432 us; the launch traced here: 430 us
  waiting for transfers between devices  264 us (61%)
  blocking collectives  92.6 us (21%)
  local copies, waits for them, and re-layouts  25.3 us (6%)
  matrix products  24.5 us (6%)
  between operations  14.1 us (3%)
  starting transfers between devices  5.32 us (1%)
    all_gather x1, waiting for transfers between devices, body(): lax.all_gather(arrived[None], 'pool', axis=0, tiled=True)  137 us
    reduce_scatter x1, waiting for transfers between devices, body(): lax.psum_scatter(jnp.einsum('jsnh,hjd->jsnd', hidden_sel, table_sel, pref...  117 us
    all_to_all x1, blocking collectives, body(): lax.all_to_all(outgoing, 'grp', split_axis=0, concat_axis=0, tiled=True)  79.1 us
    all_gather x1, blocking collectives, body(): full_rows = lax.all_gather(stream, 'cuts', axis=1, tiled=True)  13.5 us
    dot_general x1, matrix products, body(): jnp.einsum('jsnh,hjd->jsnd', hidden_sel, table_sel, preferred_element_typ...  10.9 us
    all_to_all x1, waiting for transfers between devices, body(): lax.all_to_all(reduced[0].astype(jnp.bfloat16), 'grp', split_axis=0, conc...  10.2 us
  transfers between devices with their start and end apart: 3, of which 3 were waited for; matrix products, arithmetic and copies ran while one was open for 5% of the time, Pallas kernels for 0%

commit v1 on v0

v1 whole, which is shorter than its diff:
```python
import math

import jax
import jax.numpy as jnp
from jax import lax
from jax.experimental import pallas as pl
from jax.experimental.pallas import tpu as pltpu
from jax.sharding import PartitionSpec as P

HEAD_DIM = 128
MESH = pl.DeviceIdType.MESH
OFFS = (0, 1, 5, 7, 3, 2, 6, 4)
UNITS = 8
SLOTS = 16
CW = 768
CUTS = 8
FF = 384
D = CUTS * CW
ROWS = 32
GROUPS = 4
N_SEM = 160


def attend_local(queries, key_new, value_new, key_cache, value_cache, cache_lens):
    row_count = queries.shape[0]
    kv_count = key_cache.shape[-1] // HEAD_DIM
    group_size = queries.shape[-1] // key_cache.shape[-1]
    key_span = key_cache.shape[1]
    query_part = queries.reshape(row_count, kv_count, group_size, HEAD_DIM)
    keys_part = key_cache.reshape(row_count, key_span, kv_count, HEAD_DIM)
    values_part = value_cache.reshape(row_count, key_span, kv_count, HEAD_DIM)
    knew_part = key_new.reshape(row_count, kv_count, HEAD_DIM)
    vnew_f = value_new.astype(jnp.float32).reshape(row_count, kv_count, HEAD_DIM)
    score_scale = 1.0 / math.sqrt(HEAD_DIM)
    scores = (
        jnp.einsum("rkgd,rtkd->rkgt", query_part, keys_part, preferred_element_type=jnp.float32)
        * score_scale
    )
    own_score = (
        jnp.einsum("rkgd,rkd->rkg", query_part, knew_part, preferred_element_type=jnp.float32)
        * score_scale
    )
    live_mask = (jnp.arange(key_span, dtype=jnp.int32)[None, :] < cache_lens[:, None])[
        :, None, None, :
    ]
    scores = jnp.where(live_mask, scores, -1e30)
    row_peak = jnp.maximum(jnp.max(scores, axis=-1), own_score)
    raw_weights = jnp.where(live_mask, jnp.exp(scores - row_peak[..., None]), 0.0)
    own_weight = jnp.exp(own_score - row_peak)
    denominator = jnp.sum(raw_weights, axis=-1) + own_weight
    key_probs = (raw_weights / denominator[..., None]).astype(jnp.bfloat16)
    own_prob = (own_weight / denominator).astype(jnp.bfloat16)
    head_output = jnp.einsum(
        "rkgt,rtkd->rkgd", key_probs, values_part, preferred_element_type=jnp.float32
    )
    head_output = head_output + own_prob.astype(jnp.float32)[..., None] * vnew_f[:, :, None, :]
    return head_output.reshape(row_count, -1).astype(jnp.bfloat16)


def dot(a, b):
    return jnp.dot(a, b, preferred_element_type=jnp.float32)


def moe_kernel(
    att, res, gain, disp, comb, w_in, w_out, out,
    stats, xout, xbuf, big, win, wout, hid, sib_out, sib_in, far, fwd_a, fwd_b,
    step_a, step_b, sum_a, sum_b, done, home_z, pair, home_x,
    send_sem, recv_sem, local_sem,
):
    pool, grp, cuts = lax.axis_index("pool"), lax.axis_index("grp"), lax.axis_index("cuts")
    z, x = pool * 4 + grp // 4, grp % 4
    y, k = cuts // 2, cuts % 2

    def at_z(off):
        t = (z + off) % 8
        return (t // 4, (t % 4) * 4 + x, cuts)

    def at_x(off):
        return (pool, (grp // 4) * 4 + (x + off) % 4, cuts)

    def at_cut(off):
        return (pool, grp, (cuts + off) % 8)

    sibling = (pool, grp, y * 2 + (1 - k))
    up = at_cut(2)
    down = at_cut(6)

    ys = (0, 3, 1, 2)

    def cut_of(i, other):
        core = (1 - k) if other else k
        return ((y + ys[i]) % 4) * 2 + core

    weights = []
    for c in range(CUTS):
        weights.append(
            pltpu.make_async_copy(w_in.at[0, pl.ds(c * CW, CW), :], win.at[c], local_sem.at[c])
        )
    for c in range(CUTS):
        weights.append(
            pltpu.make_async_copy(
                w_out.at[0, :, pl.ds(c * CW, CW)], wout.at[c], local_sem.at[CUTS + c]
            )
        )
    for w in weights:
        w.start()

    barrier = pltpu.get_barrier_semaphore()
    peers = [at_cut(o) for o in range(1, 8)]
    peers += [at_x(o) for o in range(1, 4)]
    peers += [at_z(o) for o in range(1, 8)]
    for peer in peers:
        pl.semaphore_signal(barrier, inc=1, device_id=peer, device_id_type=MESH)

    sent = []

    def push(src, dst, where):
        i = len(sent)
        copy = pltpu.make_async_remote_copy(
            src_ref=src,
            dst_ref=dst,
            send_sem=send_sem.at[i],
            recv_sem=recv_sem.at[i],
            device_id=where,
            device_id_type=MESH,
        )
        copy.start()
        sent.append(copy)
        return copy

    stream = (res[...].astype(jnp.float32) + att[...].astype(jnp.float32)).astype(jnp.bfloat16)
    stream = stream.astype(jnp.float32)
    total = jnp.sum(stream, axis=1, keepdims=True)
    squares = jnp.sum(stream * stream, axis=1, keepdims=True)
    lane = lax.broadcasted_iota(jnp.int32, (ROWS, 128), 1)
    stats[0] = jnp.where(lane == 0, total, squares)
    pl.semaphore_wait(barrier, len(peers))
    got = [push(stats.at[0], stats.at[o], at_cut(o)) for o in range(1, 8)]
    for g in got:
        g.wait_recv()
    sums = jnp.sum(stats[...], axis=0) * (1.0 / D)
    mean = sums[:, 0:1]
    variance = sums[:, 1:2] - mean * mean
    normed = ((stream - mean) * lax.rsqrt(variance + 1e-05) * gain[...]).astype(jnp.bfloat16)

    got_x = []
    for r in (2, 1, 3, 0):
        block = dot(disp[pl.ds(r * 64, 64), :], normed).astype(jnp.bfloat16)
        if r == 0:
            for d in range(4):
                xbuf[d, 0:SLOTS, :] = block[d * SLOTS : (d + 1) * SLOTS, :]
        else:
            for d in range(4):
                xout[r - 1, d] = block[d * SLOTS : (d + 1) * SLOTS, :]
            got_x.append(
                push(xout.at[r - 1], xbuf.at[:, pl.ds(r * SLOTS, SLOTS), :], at_x(r))
            )
    for g in got_x:
        g.wait_recv()
    got_z = [None] * UNITS
    for u in range(UNITS):
        if OFFS[u] == 0:
            big[0, u] = xbuf[0]
        else:
            got_z[u] = push(xbuf.at[OFFS[u] % 4], big.at[0, u], at_z(OFFS[u]))

    a0, a1, a2 = {}, {}, {}
    b0, b1, b2, b3, b4 = {}, {}, {}, {}, {}

    def stage_a0(u):
        if got_z[u] is not None:
            got_z[u].wait_recv()
        a0[u] = (
            push(big.at[0, u], big.at[1, u], up),
            push(big.at[0, u], big.at[2, u], down),
            push(big.at[0, u], big.at[4, u], sibling),
        )

    def stage_a1(u):
        from_down, from_up, _ = a0[u]
        from_down.wait_recv()
        first = push(big.at[1, u, pl.ds(0, 32), :], big.at[3, u, pl.ds(0, 32), :], up)
        s1 = push(big.at[1, u], big.at[5, u], sibling)
        from_up.wait_recv()
        second = push(big.at[2, u, pl.ds(32, 32), :], big.at[3, u, pl.ds(32, 32), :], down)
        s2 = push(big.at[2, u], big.at[6, u], sibling)
        a1[u] = (first, second, s1, s2)

    def stage_a2(u):
        first, second, _, _ = a1[u]
        first.wait_recv()
        second.wait_recv()
        a2[u] = push(big.at[3, u], big.at[7, u], sibling)

    def stage_mm(g):
        if g == 0:
            for w in weights[:CUTS]:
                w.wait()
        for u in (2 * g, 2 * g + 1):
            a0[u][2].wait_recv()
            a1[u][2].wait_recv()
            a1[u][3].wait_recv()
            a2[u].wait_recv()
        acc = jnp.zeros((128, FF), jnp.float32)
        for s in range(8):
            rows = big[s, 2 * g : 2 * g + 2].reshape(128, CW)
            acc = acc + dot(rows, win[cut_of(s % 4, s >= 4)])
        hid[g] = (acc / (1.0 + jnp.exp(-acc))).astype(jnp.bfloat16)

    def stage_b0(g):
        if g == 0:
            for w in weights[CUTS:]:
                w.wait()
        b0[g] = {}
        for i in (3, 2, 1, 0):
            sib_out[g, i] = dot(hid[g], wout[cut_of(i, True)]).astype(jnp.bfloat16)
            b0[g][i] = push(sib_out.at[g, i], sib_in.at[g, i], sibling)

    def chip_sum(g, i):
        b0[g][i].wait_recv()
        return dot(hid[g], wout[cut_of(i, False)]) + sib_in[g, i].astype(jnp.float32)

    def stage_b1(g):
        far[g] = chip_sum(g, 3).astype(jnp.bfloat16)
        b1[g] = (
            push(far.at[g, pl.ds(0, 64), :], fwd_a.at[g], up),
            push(far.at[g, pl.ds(64, 64), :], fwd_b.at[g], down),
        )

    def stage_b2(g):
        part = chip_sum(g, 2)
        b1[g][0].wait_recv()
        sum_a[g, 0:64] = (part[0:64] + fwd_a[g].astype(jnp.float32)).astype(jnp.bfloat16)
        sum_a[g, 64:128] = part[64:128].astype(jnp.bfloat16)
        to_up = push(sum_a.at[g], step_a.at[g], up)
        part = chip_sum(g, 1)
        b1[g][1].wait_recv()
        sum_b[g, 0:64] = part[0:64].astype(jnp.bfloat16)
        sum_b[g, 64:128] = (part[64:128] + fwd_b[g].astype(jnp.float32)).astype(jnp.bfloat16)
        to_down = push(sum_b.at[g], step_b.at[g], down)
        b2[g] = (to_up, to_down)

    def stage_b3(g):
        part = chip_sum(g, 0)
        b2[g][0].wait_recv()
        b2[g][1].wait_recv()
        part = part + step_a[g].astype(jnp.float32) + step_b[g].astype(jnp.float32)
        part = part.astype(jnp.bfloat16)
        for i in range(2):
            u = 2 * g + i
            half = part[i * 64 : (i + 1) * 64]
            if OFFS[u] == 0:
                home_z[u] = half
                b3[u] = None
            else:
                done[u] = half
                b3[u] = push(done.at[u], home_z.at[u], at_z(8 - OFFS[u]))

    def stage_b4(d):
        units = [u for u in range(UNITS) if OFFS[u] % 4 == d]
        for u in units:
            if b3[u] is not None:
                b3[u].wait_recv()
        both = home_z[units[0]].astype(jnp.float32) + home_z[units[1]].astype(jnp.float32)
        both = both.astype(jnp.bfloat16)
        home_x[0, d] = both[0:SLOTS]
        pair[d] = both
        for r in (2, 1, 3):
            b4[(r, d)] = push(
                pair.at[d, pl.ds(r * SLOTS, SLOTS), :], home_x.at[r, d], at_x(4 - r)
            )

    plan = []
    for u in range(UNITS):
        plan.append((u, stage_a0, u))
        plan.append((u + 1.2, stage_a1, u))
        plan.append((u + 2.4, stage_a2, u))
    for g in range(GROUPS):
        t = 2 * g + 1
        plan.append((t + 3.6, stage_mm, g))
        plan.append((t + 3.7, stage_b0, g))
        plan.append((t + 4.8, stage_b1, g))
        plan.append((t + 6.2, stage_b2, g))
        plan.append((t + 8.1, stage_b3, g))
    for n, d in enumerate((1, 3, 2, 0)):
        plan.append((2 * n + 12, stage_b4, d))
    for _, stage, i in sorted(plan, key=lambda p: p[0]):
        stage(i)

    for copy in b4.values():
        copy.wait_recv()
    gates = comb[...]
    high = gates.astype(jnp.bfloat16)
    low = (gates - high.astype(jnp.float32)).astype(jnp.bfloat16)
    back = home_x[...].reshape(4 * 4 * SLOTS, CW)
    out[...] = (dot(high, back) + dot(low, back)).astype(jnp.bfloat16)
    for copy in sent:
        copy.wait_send()


def body(
    residual_in,
    queries,
    key_new,
    value_new,
    key_cache,
    value_cache,
    cache_lens,
    norm_gain,
    expert_ids,
    gate_weights,
    w_in,
    w_out,
):
    attended = attend_local(queries, key_new, value_new, key_cache, value_cache, cache_lens)
    grp, cuts = lax.axis_index("grp"), lax.axis_index("cuts")
    along_x = (grp % 4 + jnp.arange(4, dtype=jnp.int32)) % 4
    along_z = (grp // 4 + jnp.arange(4, dtype=jnp.int32)) % 4
    experts = (along_z[None, :] * 4 + along_x[:, None]).reshape(16)
    picks = expert_ids[:, :, None] == experts[None, None, :]
    chosen = jnp.sum(picks.astype(jnp.int32), axis=1)
    weight_table = jnp.sum(jnp.where(picks, gate_weights[:, :, None], 0.0), axis=1)
    slot_index = jnp.cumsum(chosen, axis=0) - chosen
    dispatch = (chosen[:, :, None] == 1) & (
        slot_index[:, :, None] == jnp.arange(SLOTS, dtype=jnp.int32)[None, None, :]
    )
    combine = jnp.where(dispatch, weight_table[:, :, None], 0.0).reshape(ROWS, 16 * SLOTS)
    disp = dispatch.astype(jnp.bfloat16).reshape(ROWS, 16 * SLOTS).T
    gain = lax.dynamic_slice(norm_gain, (cuts * CW,), (CW,)).reshape(1, CW)

    vmem = pl.BlockSpec(memory_space=pltpu.VMEM)
    hbm = pl.BlockSpec(memory_space=pl.ANY)
    bf = jnp.bfloat16
    expert_mix = pl.pallas_call(
        moe_kernel,
        out_shape=jax.ShapeDtypeStruct((ROWS, CW), bf),
        in_specs=[vmem] * 5 + [hbm] * 2,
        out_specs=vmem,
        scratch_shapes=[
            pltpu.VMEM((8, ROWS, 128), jnp.float32),
            pltpu.VMEM((3, 4, SLOTS, CW), bf),
            pltpu.VMEM((4, 64, CW), bf),
            pltpu.VMEM((8, UNITS, 64, CW), bf),
            pltpu.VMEM((CUTS, CW, FF), bf),
            pltpu.VMEM((CUTS, FF, CW), bf),
            pltpu.VMEM((GROUPS, 128, FF), bf),
            pltpu.VMEM((GROUPS, 4, 128, CW), bf),
            pltpu.VMEM((GROUPS, 4, 128, CW), bf),
            pltpu.VMEM((GROUPS, 128, CW), bf),
            pltpu.VMEM((GROUPS, 64, CW), bf),
            pltpu.VMEM((GROUPS, 64, CW), bf),
            pltpu.VMEM((GROUPS, 128, CW), bf),
            pltpu.VMEM((GROUPS, 128, CW), bf),
            pltpu.VMEM((GROUPS, 128, CW), bf),
            pltpu.VMEM((GROUPS, 128, CW), bf),
            pltpu.VMEM((UNITS, 64, CW), bf),
            pltpu.VMEM((UNITS, 64, CW), bf),
            pltpu.VMEM((4, 64, CW), bf),
            pltpu.VMEM((4, 4, SLOTS, CW), bf),
            pltpu.SemaphoreType.DMA((N_SEM,)),
            pltpu.SemaphoreType.DMA((N_SEM,)),
            pltpu.SemaphoreType.DMA((2 * CUTS,)),
        ],
        compiler_params=pltpu.CompilerParams(
            collective_id=0, has_side_effects=True, vmem_limit_bytes=56 * 1024 * 1024
        ),
    )(attended, residual_in, gain, disp, combine, w_in, w_out)
    return (attended, expert_mix)


def solution(mesh):
    return jax.shard_map(
        body,
        mesh=mesh,
        in_specs=(
            P(("pool", "grp"), "cuts"),
            P(("pool", "grp"), "cuts"),
            P(("pool", "grp"), "cuts"),
            P(("pool", "grp"), "cuts"),
            P(("pool", "grp"), None, "cuts"),
            P(("pool", "grp"), None, "cuts"),
            P(("pool", "grp")),
            P(),
            P(("pool", "grp"), None),
            P(("pool", "grp"), None),
            P("grp", None, ("pool", "cuts")),
            P("grp", ("pool", "cuts"), None),
        ),
        out_specs=(P(("pool", "grp"), "cuts"), P(("pool", "grp"), "cuts")),
        check_vma=False,
    )
```

time: 432 us -> 117 us (0.27)
  waiting for transfers between devices: 264 us -> 0 us
  Pallas kernels: 0 us -> 102 us
  blocking collectives: 92.6 us -> 0 us
  matrix products: 24.5 us -> 3.25 us
  local copies, waits for them, and re-layouts: 25.3 us -> 5.69 us
  between operations: 14.1 us -> 0.71 us
  starting transfers between devices: 5.32 us -> 0 us
    all_gather x1 -> x0, waiting for transfers between devices: 137 us -> none  [body(): lax.all_gather(arrived[None], 'pool', axis=0, tiled=True)]
    reduce_scatter x1 -> x0, waiting for transfers between devices: 117 us -> none  [body(): lax.psum_scatter(jnp.einsum('jsnh,hjd->jsnd', hidden_sel, table_sel, pref...]
    pallas_call x0 -> x1, Pallas kernels: none -> 102 us  [body(): pl.pallas_call(moe_kernel, out_shape=jax.ShapeDtypeStruct((ROWS, CW), bf)...]
    all_to_all x1 -> x0, blocking collectives: 79.1 us -> none  [body(): lax.all_to_all(outgoing, 'grp', split_axis=0, concat_axis=0, tiled=True)]
    dot_general x4 -> x0, matrix products: 21.3 us -> none  [the longest x1 10.9 us: body(): jnp.einsum('jsnh,hjd->jsnd', hidden_sel, table_sel, preferred_element_typ...]
    all_gather x1 -> x0, blocking collectives: 13.5 us -> none  [body(): full_rows = lax.all_gather(stream, 'cuts', axis=1, tiled=True)]
    gather x2 -> x0, local copies, waits for them, and re-layouts: 10.9 us -> none  [the longest x1 8.21 us: body(): table_sel = jnp.take(out_table, cut_pick, axis=1)]
    all_to_all x1 -> x0, waiting for transfers between devices: 10.2 us -> none  [body(): lax.all_to_all(reduced[0].astype(jnp.bfloat16), 'grp', split_axis=0, conc...]
  transfers between devices with their start and end apart: 3 -> 0, of which waited for: 3 -> 0; matrix products, arithmetic and copies ran while one was open for 5% -> 0% of each run, Pallas kernels for 0% -> 0%
where the time goes in v1:
time: 117 us; the launch traced here: 115 us
  Pallas kernels  102 us (87%)
  local copies, waits for them, and re-layouts  5.69 us (5%)
  other arithmetic  4 us (3%)
  matrix products  3.25 us (3%)
    pallas_call x1, Pallas kernels, body(): pl.pallas_call(moe_kernel, out_shape=jax.ShapeDtypeStruct((ROWS, CW), bf)...  102 us

profile of v1, /device:TPU:2, one launch (start us, length us, event | category | flops | bytes accessed | tf_op | source)
XLA Modules:
  0.0 115.2 jit_solution(13891292334769297805)
XLA Ops:
  0.6 0.0 copy-start
  0.6 1.0 reshape.159
  1.6 0.7 iota_compare_fusion
  2.3 0.0 copy-done
  2.3 0.7 fusion.17
  3.1 0.7 convert_element_type.28
  3.8 0.9 fusion.9
  4.7 0.2 fusion.2
  4.9 1.7 %fusion.1 = bf16[32,6,128]{2,1,0:T(8,128)(2,1)S(1)} fusion(bf16[32,128,128]{2,1,0:T(8,128)(2,1)} %param.17, f32[32,6,128]{2,1,0:T(8,128)S(1)} %get-tuple-element.7, f32[32,128]{1,0:T(8,128)S(1)} %convert_element_type.28, f32[32,6]{1,0:T(8,128)S(1)} %get-tuple-element.5, f32[32,6]{1,0:T(8,128)S(1)} %get-tuple-element.4, ...), kind=kOutput, calls=%fused_computation.3 | convolution fusion | flops 6463488 | bytes 1218816 | tf_op jit(solution)/shard_map/rkgt,rtkd->rkgd/dot_general | solution.py:53
  6.5 0.6 copy.38
  7.2 0.8 dynamic_slice.3
  7.9 0.6 reshape.160.gain
  8.6 0.1 broadcast_add_fusion
  8.6 0.1 add.87
  8.7 0.8 fusion.8
  9.5 0.1 copy.30
  9.6 0.8 fusion.7
  10.4 0.1 copy.29
  10.5 0.1 copy.25
  10.5 0.1 reduce_window_sum.11
  10.6 0.1 copy.27
  10.7 0.1 copy.28
  10.8 0.1 eq.58
  10.8 0.6 broadcast_select_fusion
  11.5 0.7 copy.31.disp
  12.2 101.5 %shard_map.131 = bf16[32,768]{1,0:T(8,128)(2,1)} custom-call(bf16[32,768]{1,0:T(8,128)(2,1)} %bitcast.18, bf16[32,768]{1,0:T(8,128)(2,1)} %res.1, f32[1,768]{1,0:T(1,128)} %reshape.160.gain, bf16[256,32]{1,0:T(8,128)(2,1)} %copy.31.disp, f32[32,256]{1,0:T(8,128)} %get-tuple-element.2.comb, bf16[1,6144,384]{2,1,0:T(8,128)(2,1)} %w_in.1, ...), custom_call_target="tpu_custom_call" | custom-call | tf_op jit(solution)/shard_map/pallas_call | solution.py:334
  113.7 1.4 %copy.40 = bf16[32,768]{1,0:T(8,128)(2,1)} copy(bf16[32,768]{1,0:T(8,128)(2,1)} %shard_map.131) | data formatting | bytes 98304
  (10 shorter events, 0.1 us)
Async XLA Ops:
  0.6 1.7 %copy-start = (bf16[32,128,128]{2,1,0:T(8,128)(2,1)S(1)}, bf16[32,128,128]{2,1,0:T(8,128)(2,1)}, u32[]{:S(2)}) copy-start(bf16[32,128,128]{2,1,0:T(8,128)(2,1)} %param.16) | copy-start | bytes 3145732

commit v2 on v0

v2 whole, which is shorter than its diff:
```python
import math

import jax
import jax.numpy as jnp
from jax import lax
from jax.experimental import pallas as pl
from jax.experimental.pallas import tpu as pltpu
from jax.sharding import PartitionSpec as P

MESH = pl.DeviceIdType.MESH
BF, F32 = jnp.bfloat16, jnp.float32
OFFS = (0, 1, 7, 2, 6, 3, 5, 4)
UNITS = 8
UR = 64
ALL = UNITS * UR
SLOTS = 16
CW = 768
CUTS = 8
FF = 384
D = CUTS * CW
ROWS = 32
HEADS = 6
SPAN = 128
HD = 128
N_SEM = 160
FWD = ((0, 1), (2, 3), (4, 5), (6, 7))
BWD = ((2, 3), (4, 5), (6, 7), (1,), (0,))


def dot(a, b):
    return jnp.dot(a, b, preferred_element_type=F32)


def attention(q, knew, vnew, lens, kbuf, vbuf, kv_loads, q3, s3, o3):
    scale = 1.0 / math.sqrt(HD)
    q3[...] = jnp.zeros(q3.shape, F32)
    for h in range(HEADS):
        q3[:, h, :] = q[:, h * HD : (h + 1) * HD].astype(F32)
    new_k, new_v = knew[...].astype(F32), vnew[...].astype(F32)
    lane = lax.broadcasted_iota(jnp.int32, (8, SPAN), 1)
    for w in kv_loads[: len(kv_loads) // 2]:
        w.wait()
    own = []
    for r in range(ROWS):
        qr = q3[r]
        s = lax.dot_general(
            qr.astype(BF), kbuf[r], (((1,), (1,)), ((), ())), preferred_element_type=F32
        )
        s3[r] = jnp.where(lane < lens[r], s * scale, -1e30)
        own.append(jnp.sum(qr * new_k[r : r + 1, :], axis=1, keepdims=True) * scale)
    for w in kv_loads[len(kv_loads) // 2 :]:
        w.wait()
    for r in range(ROWS):
        s = s3[r]
        peak = jnp.maximum(jnp.max(s, axis=1, keepdims=True), own[r])
        raw = jnp.where(lane < lens[r], jnp.exp(s - peak), 0.0)
        own_raw = jnp.exp(own[r] - peak)
        total = jnp.sum(raw, axis=1, keepdims=True) + own_raw
        probs = (raw / total).astype(BF)
        own_prob = (own_raw / total).astype(BF).astype(F32)
        o3[r] = dot(probs, vbuf[r]) + own_prob * new_v[r : r + 1, :]


def routing(ids, gates, x, zl):
    j = lax.broadcasted_iota(jnp.int32, (16, ROWS), 0)
    expert = (((zl + (j & 3)) & 3) << 2) + ((x + (j >> 2)) & 3)
    chosen = jnp.zeros((16, ROWS), F32)
    weight = jnp.zeros((16, ROWS), F32)
    for t in range(4):
        hit = ids[t : t + 1, :] == expert
        chosen = chosen + jnp.where(hit, 1.0, 0.0)
        weight = weight + jnp.where(hit, gates[t : t + 1, :], 0.0)
    before = lax.broadcasted_iota(jnp.int32, (ROWS, ROWS), 0) < lax.broadcasted_iota(
        jnp.int32, (ROWS, ROWS), 1
    )
    slot = dot(chosen.astype(BF), jnp.where(before, 1.0, 0.0).astype(BF))
    spread = (lax.broadcasted_iota(jnp.int32, (256, 16), 0) >> 4) == (
        lax.broadcasted_iota(jnp.int32, (256, 16), 1)
    )
    spread = jnp.where(spread, 1.0, 0.0).astype(BF)
    high = weight.astype(BF)
    low = (weight - high.astype(F32)).astype(BF)
    place = (lax.broadcasted_iota(jnp.int32, (256, ROWS), 0) & 15).astype(F32)
    here = (dot(spread, chosen.astype(BF)) > 0.5) & (dot(spread, slot.astype(BF)) == place)
    disp = jnp.where(here, 1.0, 0.0).astype(BF)
    high = jnp.where(here, dot(spread, high), 0.0).T.astype(BF)
    low = jnp.where(here, dot(spread, low), 0.0).T.astype(BF)
    return disp, high, low


def moe_kernel(
    q, res, knew, vnew, kc, vc, lens, gain, ids, gates, w_in, w_out, out, att_out,
    kbuf, vbuf, q3, s3, o3, xout, xbuf, big, win, wout, acc, hid, sib_out, sib_in, far, fwd,
    step_a, step_b, sum_a, sum_b, done, home_z, pair, home_x,
    send_sem, recv_sem, local_sem,
):
    pool, grp, cuts = lax.axis_index("pool"), lax.axis_index("grp"), lax.axis_index("cuts")
    zl, x = grp // 4, grp % 4
    z = pool * 4 + zl
    y, k = cuts // 2, cuts % 2

    def at_z(off):
        t = (z + off) % 8
        return (t // 4, (t % 4) * 4 + x, cuts)

    def at_x(off):
        return (pool, zl * 4 + (x + off) % 4, cuts)

    sibling = (pool, grp, y * 2 + (1 - k))
    up = (pool, grp, (cuts + 2) % 8)
    down = (pool, grp, (cuts + 6) % 8)

    ys = (0, 3, 1, 2)

    def cut_of(s):
        core = k if s < 4 else 1 - k
        return ((y + ys[s % 4]) % 4) * 2 + core

    def load(src, dst, i):
        copy = pltpu.make_async_copy(src, dst, local_sem.at[i])
        copy.start()
        return copy

    kv_loads = [load(kc, kbuf, 0), load(vc, vbuf, 1)]

    barrier = pltpu.get_barrier_semaphore()
    peers = [sibling, up, down]
    peers += [at_x(o) for o in range(1, 4)]
    peers += [at_z(o) for o in range(1, 8)]
    for peer in peers:
        pl.semaphore_signal(barrier, inc=1, device_id=peer, device_id_type=MESH)

    sent, left = [], []

    def wait_left(copies):
        for copy in copies:
            copy.wait_send()
            left.append(copy)

    def push(src, dst, where):
        i = len(sent)
        copy = pltpu.make_async_remote_copy(
            src_ref=src,
            dst_ref=dst,
            send_sem=send_sem.at[i],
            recv_sem=recv_sem.at[i],
            device_id=where,
            device_id_type=MESH,
        )
        copy.start()
        sent.append(copy)
        return copy

    disp, high, low = routing(ids, gates, x, zl)
    attention(q, knew, vnew, lens, kbuf, vbuf, kv_loads, q3, s3, o3)
    in_loads = [
        load(
            w_in.at[0, pl.ds(pl.multiple_of(cut_of(s) * CW, CW), CW), :], win.at[s], 2 + s
        )
        for s in range(CUTS)
    ]
    out_loads = [
        load(
            w_out.at[0, :, pl.ds(pl.multiple_of(cut_of(s) * CW, CW), CW)], wout.at[s], 10 + s
        )
        for s in range(CUTS)
    ]
    for h in range(HEADS):
        att_out[:, h * HD : (h + 1) * HD] = o3[:, h, :].astype(BF).astype(F32)
    stream = (res[...].astype(F32) + att_out[...]).astype(BF)

    blocks = dot(disp, stream).astype(BF)
    got_x = {}
    pl.semaphore_wait(barrier, len(peers))

    def start_x(d):
        for r in range(4):
            block = blocks[(r * 4 + d) * SLOTS : (r * 4 + d + 1) * SLOTS]
            if r == 0:
                xbuf[d, 0:SLOTS, :] = block
            else:
                xout[d, r] = block
        for r in (2, 1, 3):
            got_x[d, r] = push(xout.at[d, r], xbuf.at[d, pl.ds(r * SLOTS, SLOTS), :], at_x(r))

    start_x(0)
    wait_left([got_x[0, r] for r in (1, 2, 3)])
    start_x(1)
    start_x(3)

    a0, a1, a2, got_z = {}, {}, {}, {}
    b0, b1, b2, b3, b4 = {}, {}, {}, {}, {}

    def rows_of(units):
        return units[0] * UR, len(units) * UR

    def stage_x(d):
        for r in (2, 1, 3):
            got_x[d, r].wait_recv()
        if d == 0:
            big[0, 0:UR] = xbuf[0]
        if d == 1:
            start_x(2)

    def stage_z(u):
        got_z[u] = push(xbuf.at[OFFS[u] % 4], big.at[0, pl.ds(u * UR, UR)], at_z(OFFS[u]))

    def stage_a0(u):
        if OFFS[u] != 0:
            got_z[u].wait_recv()
        at = pl.ds(u * UR, UR)
        a0[u] = (
            push(big.at[0, at], big.at[1, at], up),
            push(big.at[0, at], big.at[2, at], down),
            push(big.at[0, at], big.at[4, at], sibling),
        )

    def stage_a1(u):
        at, top, bottom = pl.ds(u * UR, UR), pl.ds(u * UR, 32), pl.ds(u * UR + 32, 32)
        from_down, from_up, _ = a0[u]
        from_down.wait_recv()
        first = push(big.at[1, top], big.at[3, top], up)
        s1 = push(big.at[1, at], big.at[5, at], sibling)
        from_up.wait_recv()
        second = push(big.at[2, bottom], big.at[3, bottom], down)
        s2 = push(big.at[2, at], big.at[6, at], sibling)
        a1[u] = (first, second, s1, s2)

    def stage_a2(u):
        first, second, _, _ = a1[u]
        first.wait_recv()
        second.wait_recv()
        at = pl.ds(u * UR, UR)
        a2[u] = push(big.at[3, at], big.at[7, at], sibling)

    def stage_mm(units):
        if units == FWD[0]:
            for w in in_loads:
                w.wait()
        for u in units:
            a0[u][2].wait_recv()
            a1[u][2].wait_recv()
            a1[u][3].wait_recv()
            a2[u].wait_recv()
        base, n = rows_of(units)
        at = slice(base, base + n)

        def add_stats(s, sums):
            total, squares = sums
            rows = big[s, at, :].astype(F32)
            for l in range(CW // 128):
                v = rows[:, l * 128 : (l + 1) * 128]
                total = total + v
                squares = squares + v * v
            return total, squares

        zero = jnp.zeros((n, 128), F32)
        total, squares = lax.fori_loop(0, CUTS, add_stats, (zero, zero))
        mean = jnp.sum(total, axis=1, keepdims=True) * (1.0 / D)
        variance = jnp.sum(squares, axis=1, keepdims=True) * (1.0 / D) - mean * mean
        scale = lax.rsqrt(variance + 1e-05)
        for s in range(CUTS):
            rows = big[s, at, :].astype(F32)
            factor = gain[:, pl.ds(pl.multiple_of(cut_of(s) * CW, CW), CW)]
            normed = ((rows - mean) * scale * factor).astype(BF)
            part = dot(normed, win[s])
            if s == 0:
                acc[0:n] = part
            elif s < CUTS - 1:
                acc[0:n] += part
        inner = acc[0:n] + part
        hid[at, :] = (inner / (1.0 + jnp.exp(-inner))).astype(BF)

    def stage_b0(units):
        if units == (1,):
            for w in out_loads:
                w.wait()
        base, n = rows_of(units)
        at = pl.ds(base, n)
        mine = hid[base : base + n]
        b0[units] = {}
        for i in (3, 2, 1, 0):
            sib_out[i, at] = dot(mine, wout[4 + i]).astype(BF)
            b0[units][i] = push(sib_out.at[i, at], sib_in.at[i, at], sibling)

    def chip_sum(units, i):
        base, n = rows_of(units)
        part = dot(hid[base : base + n], wout[i])
        b0[units][i].wait_recv()
        return part + sib_in[i, base : base + n].astype(F32)

    def stage_b1(units):
        base, n = rows_of(units)
        h = n // 2
        far[base : base + n] = chip_sum(units, 3).astype(BF)
        top, bottom = pl.ds(base, h), pl.ds(base + h, h)
        b1[units] = (
            push(far.at[top], fwd.at[top], up),
            push(far.at[bottom], fwd.at[bottom], down),
        )

    def stage_b2(units):
        base, n = rows_of(units)
        h, at = n // 2, pl.ds(base, n)
        part = chip_sum(units, 2)
        b1[units][0].wait_recv()
        sum_a[base : base + h] = (part[0:h] + fwd[base : base + h].astype(F32)).astype(BF)
        sum_a[base + h : base + n] = part[h:n].astype(BF)
        to_up = push(sum_a.at[at], step_a.at[at], up)
        part = chip_sum(units, 1)
        b1[units][1].wait_recv()
        sum_b[base : base + h] = part[0:h].astype(BF)
        sum_b[base + h : base + n] = (
            part[h:n] + fwd[base + h : base + n].astype(F32)
        ).astype(BF)
        to_down = push(sum_b.at[at], step_b.at[at], down)
        b2[units] = (to_up, to_down)

    def stage_b3(units):
        base, n = rows_of(units)
        part = chip_sum(units, 0)
        b2[units][0].wait_recv()
        b2[units][1].wait_recv()
        part = part + step_a[base : base + n].astype(F32) + step_b[base : base + n].astype(F32)
        part = part.astype(BF)
        for i, u in enumerate(units):
            half = part[i * UR : (i + 1) * UR]
            if OFFS[u] == 0:
                home_z[u] = half
            else:
                done[u] = half
                b3[u] = push(done.at[u], home_z.at[u], at_z(8 - OFFS[u]))

    def stage_b4(d):
        units = [u for u in range(UNITS) if OFFS[u] % 4 == d]
        for u in units:
            if OFFS[u] != 0:
                b3[u].wait_recv()
        both = home_z[units[0]].astype(F32) + home_z[units[1]].astype(F32)
        both = both.astype(BF)
        home_x[0, d] = both[0:SLOTS]
        pair[d] = both
        for r in (2, 1, 3):
            b4[r, d] = push(
                pair.at[d, pl.ds(r * SLOTS, SLOTS), :], home_x.at[r, d], at_x(4 - r)
            )

    plan = []
    for d, t in ((0, -1), (1, 0.1), (3, 0.2), (2, 0.3)):
        plan.append((t, stage_x, d))
    for u, t in ((1, 0.11), (2, 0.21), (3, 0.31), (4, 0.32), (5, 2.05), (6, 2.06), (7, 4.05)):
        plan.append((t, stage_z, u))
    for u in range(UNITS):
        plan.append((u, stage_a0, u))
        plan.append((u + 1.2, stage_a1, u))
        plan.append((u + 2.4, stage_a2, u))
    for units in FWD:
        plan.append((units[-1] + 3.6, stage_mm, units))
    for units, t0, t1, t2, t3 in (
        ((2, 3), 6.7, 7.8, 9.21, 11.1),
        ((4, 5), 8.7, 9.8, 11.21, 13.1),
        ((6, 7), 10.7, 11.8, 13.21, 15.1),
        ((1,), 4.7, 10.0, 13.41, 15.3),
        ((0,), 4.75, 10.1, 13.61, 15.5),
    ):
        plan.append((t0, stage_b0, units))
        plan.append((t1, stage_b1, units))
        plan.append((t2, stage_b2, units))
        plan.append((t3, stage_b3, units))
    for d, t in ((3, 15.04), (2, 15.05), (1, 16), (0, 16.1)):
        plan.append((t, stage_b4, d))
    for _, stage, i in sorted(plan, key=lambda p: p[0]):
        stage(i)

    for copy in b4.values():
        copy.wait_recv()
    back = home_x[...].reshape(4 * 4 * SLOTS, CW)
    out[...] = dot(high, back) + dot(low, back)
    for copy in sent:
        if all(copy is not c for c in left):
            copy.wait_send()


def body(
    residual_in,
    queries,
    key_new,
    value_new,
    key_cache,
    value_cache,
    cache_lens,
    norm_gain,
    expert_ids,
    gate_weights,
    w_in,
    w_out,
):
    vmem = pl.BlockSpec(memory_space=pltpu.VMEM)
    smem = pl.BlockSpec(memory_space=pltpu.SMEM)
    hbm = pl.BlockSpec(memory_space=pl.ANY)
    expert_mix, attended = pl.pallas_call(
        moe_kernel,
        out_shape=(
            jax.ShapeDtypeStruct((ROWS, CW), F32),
            jax.ShapeDtypeStruct((ROWS, CW), F32),
        ),
        in_specs=[vmem] * 4 + [hbm] * 2 + [smem] + [vmem] * 3 + [hbm] * 2,
        out_specs=(vmem, vmem),
        scratch_shapes=[
            pltpu.VMEM((ROWS, SPAN, HD), BF),
            pltpu.VMEM((ROWS, SPAN, HD), BF),
            pltpu.VMEM((ROWS, 8, HD), F32),
            pltpu.VMEM((ROWS, 8, SPAN), F32),
            pltpu.VMEM((ROWS, 8, HD), F32),
            pltpu.VMEM((4, 4, SLOTS, CW), BF),
            pltpu.VMEM((4, UR, CW), BF),
            pltpu.VMEM((CUTS, ALL, CW), BF),
            pltpu.VMEM((CUTS, CW, FF), BF),
            pltpu.VMEM((CUTS, FF, CW), BF),
            pltpu.VMEM((2 * UR, FF), F32),
            pltpu.VMEM((ALL, FF), BF),
            pltpu.VMEM((4, ALL, CW), BF),
            pltpu.VMEM((4, ALL, CW), BF),
            pltpu.VMEM((ALL, CW), BF),
            pltpu.VMEM((ALL, CW), BF),
            pltpu.VMEM((ALL, CW), BF),
            pltpu.VMEM((ALL, CW), BF),
            pltpu.VMEM((ALL, CW), BF),
            pltpu.VMEM((ALL, CW), BF),
            pltpu.VMEM((UNITS, UR, CW), BF),
            pltpu.VMEM((UNITS, UR, CW), BF),
            pltpu.VMEM((4, UR, CW), BF),
            pltpu.VMEM((4, 4, SLOTS, CW), BF),
            pltpu.SemaphoreType.DMA((N_SEM,)),
            pltpu.SemaphoreType.DMA((N_SEM,)),
            pltpu.SemaphoreType.DMA((2 + 2 * CUTS,)),
        ],
        compiler_params=pltpu.CompilerParams(
            collective_id=0, has_side_effects=True, vmem_limit_bytes=56 * 1024 * 1024
        ),
    )(
        queries,
        residual_in,
        key_new,
        value_new,
        key_cache,
        value_cache,
        cache_lens,
        norm_gain.reshape(1, D),
        expert_ids.T,
        gate_weights.T,
        w_in,
        w_out,
    )
    return (attended.astype(BF), expert_mix.astype(BF))


def solution(mesh):
    return jax.shard_map(
        body,
        mesh=mesh,
        in_specs=(
            P(("pool", "grp"), "cuts"),
            P(("pool", "grp"), "cuts"),
            P(("pool", "grp"), "cuts"),
            P(("pool", "grp"), "cuts"),
            P(("pool", "grp"), None, "cuts"),
            P(("pool", "grp"), None, "cuts"),
            P(("pool", "grp")),
            P(),
            P(("pool", "grp"), None),
            P(("pool", "grp"), None),
            P("grp", None, ("pool", "cuts")),
            P("grp", ("pool", "cuts"), None),
        ),
        out_specs=(P(("pool", "grp"), "cuts"), P(("pool", "grp"), "cuts")),
        check_vma=False,
    )
```

time: 432 us -> 99 us (0.23)
  waiting for transfers between devices: 264 us -> 0 us
  Pallas kernels: 0 us -> 95.1 us
  blocking collectives: 92.6 us -> 0 us
  local copies, waits for them, and re-layouts: 25.3 us -> 0 us
  matrix products: 24.5 us -> 0 us
  between operations: 14.1 us -> 0.64 us
  starting transfers between devices: 5.32 us -> 0 us
    all_gather x1 -> x0, waiting for transfers between devices: 137 us -> none  [body(): lax.all_gather(arrived[None], 'pool', axis=0, tiled=True)]
    reduce_scatter x1 -> x0, waiting for transfers between devices: 117 us -> none  [body(): lax.psum_scatter(jnp.einsum('jsnh,hjd->jsnd', hidden_sel, table_sel, pref...]
    pallas_call x0 -> x1, Pallas kernels: none -> 95.1 us  [body(): pl.pallas_call(moe_kernel, out_shape=(jax.ShapeDtypeStruct((ROWS, CW), F3...]
    all_to_all x1 -> x0, blocking collectives: 79.1 us -> none  [body(): lax.all_to_all(outgoing, 'grp', split_axis=0, concat_axis=0, tiled=True)]
    dot_general x7 -> x0, matrix products: 24.5 us -> none  [the longest x1 10.9 us: body(): jnp.einsum('jsnh,hjd->jsnd', hidden_sel, table_sel, preferred_element_typ...]
    all_gather x1 -> x0, blocking collectives: 13.5 us -> none  [body(): full_rows = lax.all_gather(stream, 'cuts', axis=1, tiled=True)]
    gather x2 -> x0, local copies, waits for them, and re-layouts: 10.9 us -> none  [the longest x1 8.21 us: body(): table_sel = jnp.take(out_table, cut_pick, axis=1)]
    all_to_all x1 -> x0, waiting for transfers between devices: 10.2 us -> none  [body(): lax.all_to_all(reduced[0].astype(jnp.bfloat16), 'grp', split_axis=0, conc...]
  transfers between devices with their start and end apart: 3 -> 0, of which waited for: 3 -> 0; matrix products, arithmetic and copies ran while one was open for 5% -> 0% of each run, Pallas kernels for 0% -> 0%
where the time goes in v2:
time: 99 us; the launch traced here: 98.8 us
  Pallas kernels  95.1 us (96%)
  other arithmetic  3.04 us (3%)
    pallas_call x1, Pallas kernels, body(): pl.pallas_call(moe_kernel, out_shape=(jax.ShapeDtypeStruct((ROWS, CW), F3...  95.1 us
    convert_element_type x2, other arithmetic, body(): return (attended.astype(BF), expert_mix.astype(BF))  3.04 us

profile of v2, /device:TPU:2, one launch (start us, length us, event | category | flops | bytes accessed | tf_op | source)
XLA Modules:
  0.0 98.8 jit_solution(8817109013307648994)
XLA Ops:
  0.6 95.1 %shard_map.131 = (f32[32,768]{1,0:T(8,128)}, f32[32,768]{1,0:T(8,128)}) custom-call(bf16[32,768]{1,0:T(8,128)(2,1)} %q.1, bf16[32,768]{1,0:T(8,128)(2,1)} %res.1, bf16[32,128]{1,0:T(8,128)(2,1)} %knew.1, bf16[32,128]{1,0:T(8,128)(2,1)} %vnew.1, bf16[32,128,128]{2,1,0:T(8,128)(2,1)} %kc.1, bf16[32,128,128]{2,1,0:T(8,128)(2,1)} %vc.1, s32[32]{0:T(128)} %lens.1, ...), custom_call_target="tpu_custom_call" | custom-call | tf_op jit(solution)/shard_map/pallas_call | solution.py:401
  95.7 1.5 %convert_element_type.6 = bf16[32,768]{1,0:T(8,128)(2,1)} convert(f32[32,768]{1,0:T(8,128)} %get-tuple-element.4) | non-fusion elementwise | flops 24576 | bytes 147456 | tf_op jit(solution)/shard_map/convert_element_type | solution.py:455
  97.2 1.5 %convert_element_type.7 = bf16[32,768]{1,0:T(8,128)(2,1)} convert(f32[32,768]{1,0:T(8,128)} %get-tuple-element.5) | non-fusion elementwise | flops 24576 | bytes 147456 | tf_op jit(solution)/shard_map/convert_element_type | solution.py:455

commit v3 on v2

--- a/solution.py
+++ b/solution.py
@@ -23,8 +23,19 @@
 SPAN = 128
 HD = 128
 N_SEM = 160
-FWD = ((0, 1), (2, 3), (4, 5), (6, 7))
-BWD = ((2, 3), (4, 5), (6, 7), (1,), (0,))
+PLAN = (
+    ("sx", 3), ("sx", 0), ("sx", 2), ("sx", 1), ("x", 3), ("z", 2), ("z", 5), ("x", 0), ("a0", 0),
+    ("x", 2), ("z", 4), ("z", 3), ("x", 1), ("z", 1), ("a0", 2), ("a1", 0), ("a1", 2), ("a0", 4),
+    ("z", 7), ("a0", 5), ("a1", 4), ("z", 6), ("a0", 3), ("a2", 4), ("a1", 5), ("a0", 1),
+    ("a2", 5), ("a1", 3), ("a0", 7), ("mm", (4, 5)), ("a2", 3), ("a0", 6), ("a2", 2), ("a1", 7),
+    ("a2", 0), ("b0", (4, 5)), ("b1", (4, 5)), ("mm", (2, 3)), ("a1", 6), ("a2", 7), ("a1", 1),
+    ("b0", (2, 3)), ("b2", (4, 5)), ("a2", 6), ("mm", (6, 7)), ("b1", (2, 3)), ("a2", 1),
+    ("b0", (6, 7)), ("b1", (6, 7)), ("mm", (0, 1)), ("b2", (2, 3)), ("b3", (4, 5)),
+    ("b2", (6, 7)), ("b0", (0, 1)), ("b1", (0, 1)), ("b3", (2, 3)), ("b4", 3), ("b3", (6, 7)),
+    ("b2", (0, 1)), ("b4", 2), ("b3", (0, 1)), ("b4", 1), ("b4", 0),
+)
+FIRST_MM = (4, 5)
+FIRST_B0 = (4, 5)
 
 
 def dot(a, b):
@@ -130,12 +141,7 @@
     for peer in peers:
         pl.semaphore_signal(barrier, inc=1, device_id=peer, device_id_type=MESH)
 
-    sent, left = [], []
-
-    def wait_left(copies):
-        for copy in copies:
-            copy.wait_send()
-            left.append(copy)
+    sent = []
 
     def push(src, dst, where):
         i = len(sent)
@@ -183,11 +189,6 @@
         for r in (2, 1, 3):
             got_x[d, r] = push(xout.at[d, r], xbuf.at[d, pl.ds(r * SLOTS, SLOTS), :], at_x(r))
 
-    start_x(0)
-    wait_left([got_x[0, r] for r in (1, 2, 3)])
-    start_x(1)
-    start_x(3)
-
     a0, a1, a2, got_z = {}, {}, {}, {}
     b0, b1, b2, b3, b4 = {}, {}, {}, {}, {}
 
@@ -199,8 +200,6 @@
             got_x[d, r].wait_recv()
         if d == 0:
             big[0, 0:UR] = xbuf[0]
-        if d == 1:
-            start_x(2)
 
     def stage_z(u):
         got_z[u] = push(xbuf.at[OFFS[u] % 4], big.at[0, pl.ds(u * UR, UR)], at_z(OFFS[u]))
@@ -234,7 +233,7 @@
         a2[u] = push(big.at[3, at], big.at[7, at], sibling)
 
     def stage_mm(units):
-        if units == FWD[0]:
+        if units == FIRST_MM:
             for w in in_loads:
                 w.wait()
         for u in units:
@@ -272,7 +271,7 @@
         hid[at, :] = (inner / (1.0 + jnp.exp(-inner))).astype(BF)
 
     def stage_b0(units):
-        if units == (1,):
+        if units == FIRST_B0:
             for w in out_loads:
                 w.wait()
         base, n = rows_of(units)
@@ -345,40 +344,20 @@
                 pair.at[d, pl.ds(r * SLOTS, SLOTS), :], home_x.at[r, d], at_x(4 - r)
             )
 
-    plan = []
-    for d, t in ((0, -1), (1, 0.1), (3, 0.2), (2, 0.3)):
-        plan.append((t, stage_x, d))
-    for u, t in ((1, 0.11), (2, 0.21), (3, 0.31), (4, 0.32), (5, 2.05), (6, 2.06), (7, 4.05)):
-        plan.append((t, stage_z, u))
-    for u in range(UNITS):
-        plan.append((u, stage_a0, u))
-        plan.append((u + 1.2, stage_a1, u))
-        plan.append((u + 2.4, stage_a2, u))
-    for units in FWD:
-        plan.append((units[-1] + 3.6, stage_mm, units))
-    for units, t0, t1, t2, t3 in (
-        ((2, 3), 6.7, 7.8, 9.21, 11.1),
-        ((4, 5), 8.7, 9.8, 11.21, 13.1),
-        ((6, 7), 10.7, 11.8, 13.21, 15.1),
-        ((1,), 4.7, 10.0, 13.41, 15.3),
-        ((0,), 4.75, 10.1, 13.61, 15.5),
-    ):
-        plan.append((t0, stage_b0, units))
-        plan.append((t1, stage_b1, units))
-        plan.append((t2, stage_b2, units))
-        plan.append((t3, stage_b3, units))
-    for d, t in ((3, 15.04), (2, 15.05), (1, 16), (0, 16.1)):
-        plan.append((t, stage_b4, d))
-    for _, stage, i in sorted(plan, key=lambda p: p[0]):
-        stage(i)
+    stages = {
+        "sx": start_x, "x": stage_x, "z": stage_z, "a0": stage_a0, "a1": stage_a1, "a2": stage_a2,
+        "mm": stage_mm, "b0": stage_b0, "b1": stage_b1, "b2": stage_b2, "b3": stage_b3,
+        "b4": stage_b4,
+    }
+    for name, i in PLAN:
+        stages[name](i)
 
     for copy in b4.values():
         copy.wait_recv()
     back = home_x[...].reshape(4 * 4 * SLOTS, CW)
     out[...] = dot(high, back) + dot(low, back)
     for copy in sent:
-        if all(copy is not c for c in left):
-            copy.wait_send()
+        copy.wait_send()
 
 
 def body(

time: 99 us -> 93.8 us (0.947)
  Pallas kernels: 95.1 us -> 89.9 us
    pallas_call x1, Pallas kernels: 95.1 us -> 89.9 us  [body(): pl.pallas_call(moe_kernel, out_shape=(jax.ShapeDtypeStruct((ROWS, CW), F3...]
where the time goes in v3:
time: 93.8 us; the launch traced here: 93.6 us
  Pallas kernels  89.9 us (96%)
  other arithmetic  3.04 us (3%)
    pallas_call x1, Pallas kernels, body(): pl.pallas_call(moe_kernel, out_shape=(jax.ShapeDtypeStruct((ROWS, CW), F3...  89.9 us
    convert_element_type x2, other arithmetic, body(): return (attended.astype(BF), expert_mix.astype(BF))  3.04 us

profile of v3, /device:TPU:2, one launch (start us, length us, event | category | flops | bytes accessed | tf_op | source)
XLA Modules:
  0.0 93.6 jit_solution(14437012370763106153)
XLA Ops:
  0.6 89.9 %shard_map.131 = (f32[32,768]{1,0:T(8,128)}, f32[32,768]{1,0:T(8,128)}) custom-call(bf16[32,768]{1,0:T(8,128)(2,1)} %q.1, bf16[32,768]{1,0:T(8,128)(2,1)} %res.1, bf16[32,128]{1,0:T(8,128)(2,1)} %knew.1, bf16[32,128]{1,0:T(8,128)(2,1)} %vnew.1, bf16[32,128,128]{2,1,0:T(8,128)(2,1)} %kc.1, bf16[32,128,128]{2,1,0:T(8,128)(2,1)} %vc.1, s32[32]{0:T(128)} %lens.1, ...), custom_call_target="tpu_custom_call" | custom-call | tf_op jit(solution)/shard_map/pallas_call | solution.py:380
  90.5 1.5 %convert_element_type.6 = bf16[32,768]{1,0:T(8,128)(2,1)} convert(f32[32,768]{1,0:T(8,128)} %get-tuple-element.4) | non-fusion elementwise | flops 24576 | bytes 147456 | tf_op jit(solution)/shard_map/convert_element_type | solution.py:434
  92.1 1.5 %convert_element_type.7 = bf16[32,768]{1,0:T(8,128)(2,1)} convert(f32[32,768]{1,0:T(8,128)} %get-tuple-element.5) | non-fusion elementwise | flops 24576 | bytes 147456 | tf_op jit(solution)/shard_map/convert_element_type | solution.py:434

commit v4 on v3

--- a/solution.py
+++ b/solution.py
@@ -9,7 +9,7 @@
 
 MESH = pl.DeviceIdType.MESH
 BF, F32 = jnp.bfloat16, jnp.float32
-OFFS = (0, 1, 7, 2, 6, 3, 5, 4)
+OFFS = (0, 1, 7, 3, 5, 4, 2, 6)
 UNITS = 8
 UR = 64
 ALL = UNITS * UR
@@ -22,20 +22,22 @@
 HEADS = 6
 SPAN = 128
 HD = 128
-N_SEM = 160
+N_SEND = 14
+N_RECV = 80
 PLAN = (
-    ("sx", 3), ("sx", 0), ("sx", 2), ("sx", 1), ("x", 3), ("z", 2), ("z", 5), ("x", 0), ("a0", 0),
-    ("x", 2), ("z", 4), ("z", 3), ("x", 1), ("z", 1), ("a0", 2), ("a1", 0), ("a1", 2), ("a0", 4),
-    ("z", 7), ("a0", 5), ("a1", 4), ("z", 6), ("a0", 3), ("a2", 4), ("a1", 5), ("a0", 1),
-    ("a2", 5), ("a1", 3), ("a0", 7), ("mm", (4, 5)), ("a2", 3), ("a0", 6), ("a2", 2), ("a1", 7),
-    ("a2", 0), ("b0", (4, 5)), ("b1", (4, 5)), ("mm", (2, 3)), ("a1", 6), ("a2", 7), ("a1", 1),
-    ("b0", (2, 3)), ("b2", (4, 5)), ("a2", 6), ("mm", (6, 7)), ("b1", (2, 3)), ("a2", 1),
-    ("b0", (6, 7)), ("b1", (6, 7)), ("mm", (0, 1)), ("b2", (2, 3)), ("b3", (4, 5)),
-    ("b2", (6, 7)), ("b0", (0, 1)), ("b1", (0, 1)), ("b3", (2, 3)), ("b4", 3), ("b3", (6, 7)),
-    ("b2", (0, 1)), ("b4", 2), ("b3", (0, 1)), ("b4", 1), ("b4", 0),
+    ("sx", 1), ("sx", 3), ("sx", 0), ("x", 1), ("z", 1), ("sx", 2), ("x", 3), ("z", 2), ("z", 3),
+    ("z", 4), ("x", 0), ("a0", 0), ("a0", 1), ("a0", 2), ("a1", 1), ("x", 2), ("z", 5), ("z", 6),
+    ("a1", 0), ("a1", 2), ("a0", 3), ("a2", 1), ("a2", 0), ("a0", 4), ("z", 7), ("a1", 3),
+    ("a0", 5), ("mm", (0, 1)), ("a0", 6), ("a2", 2), ("a2", 3), ("b0", (0,)), ("b0", (1,)),
+    ("a1", 4), ("a1", 5), ("a0", 7), ("mm", (2, 3)), ("b0", (2, 3)), ("a2", 4), ("a1", 6),
+    ("b1", (2, 3)), ("a2", 5), ("b1", (1,)), ("mm", (4, 5)), ("a1", 7), ("b0", (4, 5)),
+    ("b1", (4, 5)), ("b2", (2, 3)), ("b2", (4, 5)), ("a2", 6), ("a2", 7), ("mm", (6, 7)),
+    ("b1", (0,)), ("b3", (2, 3)), ("b0", (6, 7)), ("b1", (6, 7)), ("b2", (1,)), ("b3", (4, 5)),
+    ("b2", (6, 7)), ("b2", (0,)), ("b3", (1,)), ("b3", (6, 7)), ("b3", (0,)), ("b4", 3),
+    ("b4", 0), ("b4", 1), ("b4", 2),
 )
-FIRST_MM = (4, 5)
-FIRST_B0 = (4, 5)
+FIRST_MM = (0, 1)
+FIRST_B0 = (0,)
 
 
 def dot(a, b):
@@ -141,42 +143,41 @@
     for peer in peers:
         pl.semaphore_signal(barrier, inc=1, device_id=peer, device_id_type=MESH)
 
-    sent = []
-
-    def push(src, dst, where):
-        i = len(sent)
-        copy = pltpu.make_async_remote_copy(
+    sends, arrivals = {}, {}
+
+    def push(src, dst, where, stream, arrival):
+        rows = math.prod(src.shape[:-1])
+        out_at = sends.setdefault(stream, [len(sends), 0])
+        in_at = arrivals.setdefault(arrival, [len(arrivals), 0])
+        out_at[1] += rows
+        in_at[1] += rows
+        pltpu.make_async_remote_copy(
             src_ref=src,
             dst_ref=dst,
-            send_sem=send_sem.at[i],
-            recv_sem=recv_sem.at[i],
+            send_sem=send_sem.at[out_at[0]],
+            recv_sem=recv_sem.at[in_at[0]],
             device_id=where,
             device_id_type=MESH,
-        )
-        copy.start()
-        sent.append(copy)
-        return copy
+        ).start()
+
+    def block_of(rows):
+        return big.at[0, pl.ds(0, rows)] if rows <= ALL else sib_out.at[pl.ds(0, rows // ALL)]
+
+    def arrived(key):
+        at, rows = arrivals[key]
+        pltpu.make_async_copy(block_of(rows), block_of(rows), recv_sem.at[at]).wait()
 
     disp, high, low = routing(ids, gates, x, zl)
     attention(q, knew, vnew, lens, kbuf, vbuf, kv_loads, q3, s3, o3)
-    in_loads = [
-        load(
-            w_in.at[0, pl.ds(pl.multiple_of(cut_of(s) * CW, CW), CW), :], win.at[s], 2 + s
-        )
-        for s in range(CUTS)
-    ]
-    out_loads = [
-        load(
-            w_out.at[0, :, pl.ds(pl.multiple_of(cut_of(s) * CW, CW), CW)], wout.at[s], 10 + s
-        )
-        for s in range(CUTS)
-    ]
+    for s in range(CUTS):
+        load(w_in.at[0, pl.ds(pl.multiple_of(cut_of(s) * CW, CW), CW), :], win.at[s], 2)
+    for s in range(CUTS):
+        load(w_out.at[0, :, pl.ds(pl.multiple_of(cut_of(s) * CW, CW), CW)], wout.at[s], 3)
     for h in range(HEADS):
         att_out[:, h * HD : (h + 1) * HD] = o3[:, h, :].astype(BF).astype(F32)
     stream = (res[...].astype(F32) + att_out[...]).astype(BF)
 
     blocks = dot(disp, stream).astype(BF)
-    got_x = {}
     pl.semaphore_wait(barrier, len(peers))
 
     def start_x(d):
@@ -187,60 +188,50 @@
             else:
                 xout[d, r] = block
         for r in (2, 1, 3):
-            got_x[d, r] = push(xout.at[d, r], xbuf.at[d, pl.ds(r * SLOTS, SLOTS), :], at_x(r))
-
-    a0, a1, a2, got_z = {}, {}, {}, {}
-    b0, b1, b2, b3, b4 = {}, {}, {}, {}, {}
+            push(
+                xout.at[d, r], xbuf.at[d, pl.ds(r * SLOTS, SLOTS), :], at_x(r), "x", ("x", d)
+            )
 
     def rows_of(units):
         return units[0] * UR, len(units) * UR
 
     def stage_x(d):
-        for r in (2, 1, 3):
-            got_x[d, r].wait_recv()
+        arrived(("x", d))
         if d == 0:
             big[0, 0:UR] = xbuf[0]
 
     def stage_z(u):
-        got_z[u] = push(xbuf.at[OFFS[u] % 4], big.at[0, pl.ds(u * UR, UR)], at_z(OFFS[u]))
+        push(xbuf.at[OFFS[u] % 4], big.at[0, pl.ds(u * UR, UR)], at_z(OFFS[u]), "z", ("z", u))
+
+    def to_sibling(i, u):
+        at = pl.ds(u * UR, UR)
+        push(big.at[i, at], big.at[4 + i, at], sibling, "s", ("s", u // 2))
 
     def stage_a0(u):
         if OFFS[u] != 0:
-            got_z[u].wait_recv()
+            arrived(("z", u))
         at = pl.ds(u * UR, UR)
-        a0[u] = (
-            push(big.at[0, at], big.at[1, at], up),
-            push(big.at[0, at], big.at[2, at], down),
-            push(big.at[0, at], big.at[4, at], sibling),
-        )
+        push(big.at[0, at], big.at[1, at], up, "u", ("u", u))
+        push(big.at[0, at], big.at[2, at], down, "d", ("d", u))
+        to_sibling(0, u)
 
     def stage_a1(u):
-        at, top, bottom = pl.ds(u * UR, UR), pl.ds(u * UR, 32), pl.ds(u * UR + 32, 32)
-        from_down, from_up, _ = a0[u]
-        from_down.wait_recv()
-        first = push(big.at[1, top], big.at[3, top], up)
-        s1 = push(big.at[1, at], big.at[5, at], sibling)
-        from_up.wait_recv()
-        second = push(big.at[2, bottom], big.at[3, bottom], down)
-        s2 = push(big.at[2, at], big.at[6, at], sibling)
-        a1[u] = (first, second, s1, s2)
+        top, bottom = pl.ds(u * UR, 32), pl.ds(u * UR + 32, 32)
+        arrived(("u", u))
+        push(big.at[1, top], big.at[3, top], up, "f", ("f", u))
+        to_sibling(1, u)
+        arrived(("d", u))
+        push(big.at[2, bottom], big.at[3, bottom], down, "g", ("f", u))
+        to_sibling(2, u)
 
     def stage_a2(u):
-        first, second, _, _ = a1[u]
-        first.wait_recv()
-        second.wait_recv()
-        at = pl.ds(u * UR, UR)
-        a2[u] = push(big.at[3, at], big.at[7, at], sibling)
+        arrived(("f", u))
+        to_sibling(3, u)
 
     def stage_mm(units):
         if units == FIRST_MM:
-            for w in in_loads:
-                w.wait()
-        for u in units:
-            a0[u][2].wait_recv()
-            a1[u][2].wait_recv()
-            a1[u][3].wait_recv()
-            a2[u].wait_recv()
+            pltpu.make_async_copy(win, win, local_sem.at[2]).wait()
+        arrived(("s", units[0] // 2))
         base, n = rows_of(units)
         at = slice(base, base + n)
 
@@ -272,20 +263,18 @@
 
     def stage_b0(units):
         if units == FIRST_B0:
-            for w in out_loads:
-                w.wait()
+            pltpu.make_async_copy(wout, wout, local_sem.at[3]).wait()
         base, n = rows_of(units)
         at = pl.ds(base, n)
         mine = hid[base : base + n]
-        b0[units] = {}
         for i in (3, 2, 1, 0):
             sib_out[i, at] = dot(mine, wout[4 + i]).astype(BF)
-            b0[units][i] = push(sib_out.at[i, at], sib_in.at[i, at], sibling)
+            push(sib_out.at[i, at], sib_in.at[i, at], sibling, "b", ("b", units, i))
 
     def chip_sum(units, i):
         base, n = rows_of(units)
         part = dot(hid[base : base + n], wout[i])
-        b0[units][i].wait_recv()
+        arrived(("b", units, i))
         return part + sib_in[i, base : base + n].astype(F32)
 
     def stage_b1(units):
@@ -293,33 +282,29 @@
         h = n // 2
         far[base : base + n] = chip_sum(units, 3).astype(BF)
         top, bottom = pl.ds(base, h), pl.ds(base + h, h)
-        b1[units] = (
-            push(far.at[top], fwd.at[top], up),
-            push(far.at[bottom], fwd.at[bottom], down),
-        )
+        push(far.at[top], fwd.at[top], up, "fa", ("fa", units))
+        push(far.at[bottom], fwd.at[bottom], down, "fb", ("fb", units))
 
     def stage_b2(units):
         base, n = rows_of(units)
         h, at = n // 2, pl.ds(base, n)
         part = chip_sum(units, 2)
-        b1[units][0].wait_recv()
+        arrived(("fa", units))
         sum_a[base : base + h] = (part[0:h] + fwd[base : base + h].astype(F32)).astype(BF)
         sum_a[base + h : base + n] = part[h:n].astype(BF)
-        to_up = push(sum_a.at[at], step_a.at[at], up)
+        push(sum_a.at[at], step_a.at[at], up, "ga", ("g", units))
         part = chip_sum(units, 1)
-        b1[units][1].wait_recv()
+        arrived(("fb", units))
         sum_b[base : base + h] = part[0:h].astype(BF)
         sum_b[base + h : base + n] = (
             part[h:n] + fwd[base + h : base + n].astype(F32)
         ).astype(BF)
-        to_down = push(sum_b.at[at], step_b.at[at], down)
-        b2[units] = (to_up, to_down)
+        push(sum_b.at[at], step_b.at[at], down, "gb", ("g", units))
 
     def stage_b3(units):
         base, n = rows_of(units)
         part = chip_sum(units, 0)
-        b2[units][0].wait_recv()
-        b2[units][1].wait_recv()
+        arrived(("g", units))
         part = part + step_a[base : base + n].astype(F32) + step_b[base : base + n].astype(F32)
         part = part.astype(BF)
         for i, u in enumerate(units):
@@ -328,20 +313,18 @@
                 home_z[u] = half
             else:
                 done[u] = half
-                b3[u] = push(done.at[u], home_z.at[u], at_z(8 - OFFS[u]))
+                push(done.at[u], home_z.at[u], at_z(8 - OFFS[u]), "h", ("h", OFFS[u] % 4))
 
     def stage_b4(d):
         units = [u for u in range(UNITS) if OFFS[u] % 4 == d]
-        for u in units:
-            if OFFS[u] != 0:
-                b3[u].wait_recv()
+        arrived(("h", d))
         both = home_z[units[0]].astype(F32) + home_z[units[1]].astype(F32)
         both = both.astype(BF)
         home_x[0, d] = both[0:SLOTS]
         pair[d] = both
         for r in (2, 1, 3):
-            b4[r, d] = push(
-                pair.at[d, pl.ds(r * SLOTS, SLOTS), :], home_x.at[r, d], at_x(4 - r)
+            push(
+                pair.at[d, pl.ds(r * SLOTS, SLOTS), :], home_x.at[r, d], at_x(4 - r), "hx", "hx"
             )
 
     stages = {
@@ -352,12 +335,11 @@
     for name, i in PLAN:
         stages[name](i)
 
-    for copy in b4.values():
-        copy.wait_recv()
+    arrived("hx")
     back = home_x[...].reshape(4 * 4 * SLOTS, CW)
     out[...] = dot(high, back) + dot(low, back)
-    for copy in sent:
-        copy.wait_send()
+    for at, rows in sends.values():
+        pltpu.make_async_copy(block_of(rows), block_of(rows), send_sem.at[at]).wait()
 
 
 def body(
@@ -410,9 +392,9 @@
             pltpu.VMEM((UNITS, UR, CW), BF),
             pltpu.VMEM((4, UR, CW), BF),
             pltpu.VMEM((4, 4, SLOTS, CW), BF),
-            pltpu.SemaphoreType.DMA((N_SEM,)),
-            pltpu.SemaphoreType.DMA((N_SEM,)),
-            pltpu.SemaphoreType.DMA((2 + 2 * CUTS,)),
+            pltpu.SemaphoreType.DMA((N_SEND,)),
+            pltpu.SemaphoreType.DMA((N_RECV,)),
+            pltpu.SemaphoreType.DMA((4,)),
         ],
         compiler_params=pltpu.CompilerParams(
             collective_id=0, has_side_effects=True, vmem_limit_bytes=56 * 1024 * 1024

time: 93.8 us -> 86.4 us (0.921)
  the two profiles are of different devices: /device:TPU:2 before, /device:TPU:32 now
where the time goes in v4:
time: 86.4 us; the launch traced here: 86.1 us
  Pallas kernels  82.4 us (95%)
  other arithmetic  3.04 us (4%)
    pallas_call x1, Pallas kernels, body(): pl.pallas_call(moe_kernel, out_shape=(jax.ShapeDtypeStruct((ROWS, CW), F3...  82.4 us
    convert_element_type x2, other arithmetic, body(): return (attended.astype(BF), expert_mix.astype(BF))  3.04 us

profile of v4, /device:TPU:32, one launch (start us, length us, event | category | flops | bytes accessed | tf_op | source)
XLA Modules:
  0.0 86.1 jit_solution(9097805334098612283)
XLA Ops:
  0.6 82.4 %shard_map.131 = (f32[32,768]{1,0:T(8,128)}, f32[32,768]{1,0:T(8,128)}) custom-call(bf16[32,768]{1,0:T(8,128)(2,1)} %q.1, bf16[32,768]{1,0:T(8,128)(2,1)} %res.1, bf16[32,128]{1,0:T(8,128)(2,1)} %knew.1, bf16[32,128]{1,0:T(8,128)(2,1)} %vnew.1, bf16[32,128,128]{2,1,0:T(8,128)(2,1)} %kc.1, bf16[32,128,128]{2,1,0:T(8,128)(2,1)} %vc.1, s32[32]{0:T(128)} %lens.1, ...), custom_call_target="tpu_custom_call" | custom-call | tf_op jit(solution)/shard_map/pallas_call | solution.py:362
  83.1 1.5 %convert_element_type.6 = bf16[32,768]{1,0:T(8,128)(2,1)} convert(f32[32,768]{1,0:T(8,128)} %get-tuple-element.4) | non-fusion elementwise | flops 24576 | bytes 147456 | tf_op jit(solution)/shard_map/convert_element_type | solution.py:416
  84.6 1.5 %convert_element_type.7 = bf16[32,768]{1,0:T(8,128)(2,1)} convert(f32[32,768]{1,0:T(8,128)} %get-tuple-element.5) | non-fusion elementwise | flops 24576 | bytes 147456 | tf_op jit(solution)/shard_map/convert_element_type | solution.py:416

commit v5 on v4

--- a/solution.py
+++ b/solution.py
@@ -25,19 +25,19 @@
 N_SEND = 14
 N_RECV = 80
 PLAN = (
-    ("sx", 1), ("sx", 3), ("sx", 0), ("x", 1), ("z", 1), ("sx", 2), ("x", 3), ("z", 2), ("z", 3),
-    ("z", 4), ("x", 0), ("a0", 0), ("a0", 1), ("a0", 2), ("a1", 1), ("x", 2), ("z", 5), ("z", 6),
-    ("a1", 0), ("a1", 2), ("a0", 3), ("a2", 1), ("a2", 0), ("a0", 4), ("z", 7), ("a1", 3),
-    ("a0", 5), ("mm", (0, 1)), ("a0", 6), ("a2", 2), ("a2", 3), ("b0", (0,)), ("b0", (1,)),
-    ("a1", 4), ("a1", 5), ("a0", 7), ("mm", (2, 3)), ("b0", (2, 3)), ("a2", 4), ("a1", 6),
-    ("b1", (2, 3)), ("a2", 5), ("b1", (1,)), ("mm", (4, 5)), ("a1", 7), ("b0", (4, 5)),
-    ("b1", (4, 5)), ("b2", (2, 3)), ("b2", (4, 5)), ("a2", 6), ("a2", 7), ("mm", (6, 7)),
-    ("b1", (0,)), ("b3", (2, 3)), ("b0", (6, 7)), ("b1", (6, 7)), ("b2", (1,)), ("b3", (4, 5)),
-    ("b2", (6, 7)), ("b2", (0,)), ("b3", (1,)), ("b3", (6, 7)), ("b3", (0,)), ("b4", 3),
-    ("b4", 0), ("b4", 1), ("b4", 2),
+    ("sx", 3), ("sx", 0), ("sx", 1), ("x", 3), ("z", 2), ("z", 3), ("x", 0), ("a0", 0), ("x", 1),
+    ("z", 4), ("a0", 2), ("z", 1), ("sx", 2), ("z", 5), ("a1", 0), ("a1", 2), ("a0", 3), ("x", 2),
+    ("a0", 4), ("z", 6), ("z", 7), ("a1", 3), ("a0", 1), ("a1", 4), ("a0", 5), ("a2", 3),
+    ("a2", 2), ("a0", 6), ("mm", (2, 3)), ("a1", 5), ("b0", (2, 3)), ("a0", 7), ("a1", 1),
+    ("a2", 4), ("b1", (2, 3)), ("a2", 0), ("a1", 6), ("a2", 5), ("mm", (4, 5)), ("a1", 7),
+    ("b0", (4, 5)), ("a2", 1), ("b1", (4, 5)), ("b2", (2, 3)), ("a2", 6), ("mm", (0, 1)),
+    ("a2", 7), ("b0", (0,)), ("b2", (4, 5)), ("mm", (6, 7)), ("b0", (1,)), ("b0", (6, 7)),
+    ("b1", (1,)), ("b3", (2, 3)), ("b1", (6, 7)), ("b3", (4, 5)), ("b2", (1,)), ("b2", (6, 7)),
+    ("b4", 3), ("b3", (1,)), ("b1", (0,)), ("b3", (6, 7)), ("b2", (0,)), ("b4", 1), ("b3", (0,)),
+    ("b4", 0), ("b4", 2),
 )
-FIRST_MM = (0, 1)
-FIRST_B0 = (0,)
+FIRST_MM = (2, 3)
+FIRST_B0 = (2, 3)
 
 
 def dot(a, b):
@@ -174,8 +174,8 @@
     for s in range(CUTS):
         load(w_out.at[0, :, pl.ds(pl.multiple_of(cut_of(s) * CW, CW), CW)], wout.at[s], 3)
     for h in range(HEADS):
-        att_out[:, h * HD : (h + 1) * HD] = o3[:, h, :].astype(BF).astype(F32)
-    stream = (res[...].astype(F32) + att_out[...]).astype(BF)
+        att_out[:, h * HD : (h + 1) * HD] = o3[:, h, :].astype(BF)
+    stream = (res[...].astype(F32) + att_out[...].astype(F32)).astype(BF)
 
     blocks = dot(disp, stream).astype(BF)
     pl.semaphore_wait(barrier, len(peers))
@@ -337,7 +337,7 @@
 
     arrived("hx")
     back = home_x[...].reshape(4 * 4 * SLOTS, CW)
-    out[...] = dot(high, back) + dot(low, back)
+    out[...] = (dot(high, back) + dot(low, back)).astype(BF)
     for at, rows in sends.values():
         pltpu.make_async_copy(block_of(rows), block_of(rows), send_sem.at[at]).wait()
 
@@ -362,8 +362,8 @@
     expert_mix, attended = pl.pallas_call(
         moe_kernel,
         out_shape=(
-            jax.ShapeDtypeStruct((ROWS, CW), F32),
-            jax.ShapeDtypeStruct((ROWS, CW), F32),
+            jax.ShapeDtypeStruct((ROWS, CW), BF),
+            jax.ShapeDtypeStruct((ROWS, CW), BF),
         ),
         in_specs=[vmem] * 4 + [hbm] * 2 + [smem] + [vmem] * 3 + [hbm] * 2,
         out_specs=(vmem, vmem),
@@ -413,7 +413,7 @@
         w_in,
         w_out,
     )
-    return (attended.astype(BF), expert_mix.astype(BF))
+    return (attended, expert_mix)
 
 
 def solution(mesh):

time: 86.4 us -> 87.1 us (level)
  the two profiles are of different devices: /device:TPU:32 before, /device:TPU:2 now
where the time goes in v5:
time: 87.1 us; the launch traced here: 86.8 us
  Pallas kernels  83.3 us (96%)
  local copies, waits for them, and re-layouts  2.84 us (3%)
    pallas_call x1, Pallas kernels, body(): pl.pallas_call(moe_kernel, out_shape=(jax.ShapeDtypeStruct((ROWS, CW), BF...  83.3 us
    unnamed x2, local copies, waits for them, and re-layouts  2.84 us

profile of v5, /device:TPU:2, one launch (start us, length us, event | category | flops | bytes accessed | tf_op | source)
XLA Modules:
  0.0 86.8 jit_solution(4431560316743757893)
XLA Ops:
  0.6 83.3 %shard_map.131 = (bf16[32,768]{1,0:T(8,128)(2,1)}, bf16[32,768]{1,0:T(8,128)(2,1)}) custom-call(bf16[32,768]{1,0:T(8,128)(2,1)} %q.1, bf16[32,768]{1,0:T(8,128)(2,1)} %res.1, bf16[32,128]{1,0:T(8,128)(2,1)} %knew.1, bf16[32,128]{1,0:T(8,128)(2,1)} %vnew.1, bf16[32,128,128]{2,1,0:T(8,128)(2,1)} %kc.1, bf16[32,128,128]{2,1,0:T(8,128)(2,1)} %vc.1, s32[32]{0:T(128)} %lens.1, ...), custom_call_target="tpu_custom_call" | custom-call | tf_op jit(solution)/shard_map/pallas_call | solution.py:362
  84.0 1.4 %copy.16 = bf16[32,768]{1,0:T(8,128)(2,1)} copy(bf16[32,768]{1,0:T(8,128)(2,1)} %get-tuple-element.8) | data formatting | bytes 98304
  85.4 1.4 %copy.17 = bf16[32,768]{1,0:T(8,128)(2,1)} copy(bf16[32,768]{1,0:T(8,128)(2,1)} %get-tuple-element.9) | data formatting | bytes 98304
